TPU v7x, 256 devices: a whole 4x4x8 slice. The times are simulated.
256 devices in a mesh: src: 32 (over x, z), tgt: 8 (over y, core).
Axes of the slice: x: 4, y: 4, z: 8, core: 2. Of those that a mesh axis runs over, the one named last changes fastest.
Arguments:
- src_points: float32 [16384, 32], P(('src', 'tgt')), may hold values from -4.5 to 4.5
- log_a: float32 [16384], P(('src', 'tgt')), may hold values from -1 to 1
- tgt_points: float32 [65536, 32], P(('src', 'tgt')), may hold values from -1.5 to 1.5
- log_b: float32 [65536], P(('src', 'tgt')), may hold values from -1 to 1
- g_init: float32 [65536], P(('src', 'tgt')), may hold values from -60 to 1.5
Outputs:
- f_pot: float32 [16384], P(('src', 'tgt'))
- g_pot: float32 [65536], P(('src', 'tgt'))
All inputs are finite; a program needn't handle non-finite values.
Results may differ from a plain program's by a relative error of at most 0.0003.
Values sent between devices are 32-bit elements; how exact they have to be, the bound alone decides.
No kernel may reach another device: no remote copies, remote signals or barrier semaphores. Data moves between devices by JAX's collectives and lax.ppermute only.
A program may use at most 64 MiB of HBM per device.

v0:
```python
import jax
import jax.numpy as jnp
import numpy as np
from jax import lax
from jax.experimental import pallas as pl
from jax.experimental.pallas import tpu as pltpu
from jax.sharding import Mesh
from jax.sharding import PartitionSpec as P

EPSILON = 0.5
LOG2E = float(np.log2(np.e))
LN2 = float(np.log(2.0))
AXES = ("x", "z", "y", "c")
SOURCE_AXES = ("y", "x")
TARGET_AXES = ("c", "z")
DIM = 32
PACK = DIM // 2 + 8
DEPTH = 128
VEC = 3 * DIM
TILE = 256
CHUNK = 128
OVERFLOW = 1e38
F32 = jnp.float32
BF16 = jnp.bfloat16
Z_ORDER = (0, 4, 1, 5, 2, 6, 3, 7)
JOIN_COST = pl.CostEstimate(flops=1000000000000, bytes_accessed=0, transcendentals=0)


def split(v, count):
    pieces = []
    for _ in range(count):
        piece = v.astype(BF16)
        pieces.append(piece.astype(F32))
        v = v - pieces[-1]
    return pieces


def vector_rows(first, second, width):
    def rows(v):
        if v is None:
            return [jnp.ones((1, width), F32)] * 3
        return split(v, 3)

    zeros = jnp.zeros((10, width), F32)
    return jnp.concatenate(rows(first) + rows(second) + [zeros], axis=0).astype(BF16)


def flat(dense):
    return jnp.concatenate([dense[r : r + 1] for r in range(dense.shape[0])], axis=1)


def combine(parts):
    top = jnp.max(parts, axis=0)
    return top + jnp.log2(jnp.sum(jnp.exp2(parts - top[None]), axis=0))


def lse_pass(lhs_t, lhs_ref, rhs_ref, write):
    largest = None
    for at in range(0, rhs_ref.shape[1], TILE):
        rhs = rhs_ref[:, at : at + TILE]
        top = total = None
        for row in range(0, lhs_ref.shape[0], CHUNK):
            if at == 0:
                lhs = lhs_t[:, row : row + CHUNK].T
                lhs_ref[row : row + CHUNK, :] = lhs
            else:
                lhs = lhs_ref[row : row + CHUNK, :]
            terms = jnp.dot(lhs, rhs, preferred_element_type=F32).reshape(CHUNK // 8, 8, TILE)
            if top is None:
                top = jnp.max(jnp.max(terms, axis=0), axis=0, keepdims=True)
            added = jnp.sum(jnp.exp2(terms - top[None]), axis=0)
            total = added if total is None else total + added
        total = jnp.sum(total, axis=0, keepdims=True)
        largest = total if largest is None else jnp.maximum(largest, total)
        write(at // TILE, top + jnp.log2(total))

    @pl.when(jnp.logical_not(jnp.max(largest) < OVERFLOW))
    def _():
        running_lse_pass(lhs_ref, rhs_ref, write)


def running_lse_pass(lhs_ref, rhs_ref, write):
    def tile(n, carry):
        rhs = rhs_ref[:, pl.ds(pl.multiple_of(n * TILE, TILE), TILE)]

        def step(r, state):
            top, total = state
            lhs = lhs_ref[pl.ds(pl.multiple_of(r * CHUNK, CHUNK), CHUNK), :]
            terms = jnp.dot(lhs, rhs, preferred_element_type=F32).reshape(CHUNK // 8, 8, TILE)
            newtop = jnp.maximum(top, jnp.max(terms, axis=0))
            added = jnp.sum(jnp.exp2(terms - newtop[None]), axis=0)
            return newtop, total * jnp.exp2(top - newtop) + added

        start = (jnp.full((8, TILE), -1e30, F32), jnp.zeros((8, TILE), F32))
        top, total = lax.fori_loop(0, lhs_ref.shape[0] // CHUNK, step, start, unroll=8)
        peak = jnp.max(top, axis=0, keepdims=True)
        total = jnp.sum(total * jnp.exp2(top - peak), axis=0, keepdims=True)
        write(n, peak + jnp.log2(total))
        return carry

    lax.fori_loop(0, rhs_ref.shape[1] // TILE, tile, 0)


def write_dense(out_ref):
    copies, _, width = out_ref.shape
    step = min(TILE, width)

    def write(n, value):
        for at in range(0, TILE, step):
            start = n * TILE + at
            row, lane = start // width, start % width
            lane = lane if isinstance(n, int) else pl.multiple_of(lane, step)
            piece = value[None, :, at : at + step]
            out_ref[:, pl.ds(row, 1), pl.ds(lane, step)] = jnp.broadcast_to(piece, (copies, 1, step))

    return write


def pack_kernel(src_hbm, la_hbm, tgt_hbm, lb_hbm, g_hbm, spack, tpack, ssq, tsq, src, la, tgt, lb, g, sems):
    pairs = ((src_hbm, src), (la_hbm, la), (tgt_hbm, tgt), (lb_hbm, lb), (g_hbm, g))
    copies = [pltpu.make_async_copy(a, b, sems.at[i]) for i, (a, b) in enumerate(pairs)]
    for copy in copies:
        copy.start()
    for copy in copies:
        copy.wait()
    s_t, t_t = src[...], tgt[...]
    s_norm = jnp.sum(s_t * s_t, axis=0, keepdims=True)
    t_norm = jnp.sum(t_t * t_t, axis=0, keepdims=True)
    ssq[...] = s_norm
    tsq[...] = t_norm
    s_t = s_t * ((2.0 / EPSILON) * LOG2E)
    weights = jnp.concatenate([la[...] * LOG2E, jnp.zeros_like(la[...])], axis=1)
    spack[: DIM // 2] = jnp.concatenate([s_t[: DIM // 2], s_t[DIM // 2 :]], axis=1)
    spack[DIM // 2 :] = jnp.broadcast_to(weights, (PACK - DIM // 2, weights.shape[1]))
    h = (lb[...] + (g[...] - t_norm) / EPSILON) * LOG2E
    weights = lb[...] * LOG2E
    half = t_t.shape[1] // 2
    rows = [t_t[:, :half], t_t[:, half:], h[:, :half], h[:, half:], weights[:, :half], weights[:, half:]]
    packed = jnp.concatenate(rows + [jnp.zeros((4, half), F32)], axis=0)
    tpack[...] = jnp.broadcast_to(packed[None], tpack.shape)


def join_kernel(first, second, out):
    rows = first.shape[0]
    out[:rows] = first[...]
    out[rows:] = second[...]


def first_kernel(mine, other, tpg_hbm, out, akm, bkm, la, lb, brm, bh, packs, tpg, sem):
    copy = pltpu.make_async_copy(tpg_hbm, tpg, sem)
    copy.start()
    own = mine.shape[1] // 2
    half = DIM // 2
    me = lax.axis_index(TARGET_AXES)
    for at, offset in enumerate(Z_ORDER):
        row = slice(PACK * at, PACK * (at + 1))
        packs[offset], packs[offset + 8] = mine[row], other[row]
    pieces = []
    for p in range(0, packs.shape[0], 2):
        a, b = packs[p ^ me], packs[(p + 1) ^ me]
        top = jnp.concatenate([a[:, :own], b[:, :own]], axis=1)
        low = jnp.concatenate([a[:half, own:], b[:half, own:]], axis=1)
        la[:, own * p : own * (p + 2)] = top[half : half + 1]
        pieces.append(jnp.concatenate([top[:half], low], axis=0))
    s = jnp.concatenate(pieces, axis=1)
    s1, s2 = (v.astype(BF16) for v in split(s, 2))
    width = s.shape[1]
    none = jnp.zeros((1, width), F32)
    akm[...] = jnp.concatenate([s1, s1, s2, vector_rows(none, None, width), jnp.zeros((16, width), BF16)], axis=0)
    copy.wait()
    width = 2 * tpg.shape[2]
    none = jnp.zeros((1, width), F32)
    zeros = jnp.zeros((16, width), BF16)
    for p in range(tpg.shape[0]):
        at = slice(width * p, width * (p + 1))
        wide = lambda row, count: jnp.concatenate([tpg[p, row : row + count], tpg[p, row + count : row + 2 * count]], axis=1)
        t1, t2 = (v.astype(BF16) for v in split(wide(0, DIM), 2))
        h = wide(2 * DIM, 1)
        lb[:, at] = wide(2 * DIM + 2, 1)
        bkm[:, at] = jnp.concatenate([t1, t2, t1, vector_rows(None, none, width), zeros], axis=0)
        bh[:, at] = jnp.concatenate([t1, t2, t1, vector_rows(None, h, width), zeros], axis=0)
    lse_pass(bh, brm, akm, write_dense(out))


def column_kernel(parts, la, akm, bkm, out, arm, tmp):
    k = la[...] - flat(combine(parts[...]))
    tmp[...] = akm[...]
    tmp[VEC : VEC + 16, :] = vector_rows(k, None, k.shape[1])
    lse_pass(tmp, arm, bkm, write_dense(out))


def row_kernel(parts, lb, akm, bkm, out, brm, tmp):
    h = lb[...] - flat(combine(parts[...]))
    tmp[...] = bkm[...]
    tmp[VEC : VEC + 16, :] = vector_rows(None, h, h.shape[1])
    lse_pass(tmp, brm, akm, write_dense(out))


def last_column_kernel(parts, la, akm, bkm, out, own_rows, arm, tmp):
    rows = flat(combine(parts[...]))
    me = lax.axis_index(TARGET_AXES)
    own = own_rows.shape[1]
    mine = jnp.zeros((1, own), F32)
    for p in range(rows.shape[1] // own):
        mine = mine + jnp.where(me == p, rows[:, own * p : own * (p + 1)], 0.0)
    own_rows[...] = mine
    k = la[...] - rows
    tmp[...] = akm[...]
    tmp[VEC : VEC + 16, :] = vector_rows(k, None, k.shape[1])

    def write(n, value):
        out[n] = value

    lse_pass(tmp, arm, bkm, write)


def last_kernel(parts, own_rows, ssq, tsq, f, g):
    f[...] = ssq[...] - (EPSILON * LN2) * own_rows[...]
    g[...] = tsq[...] - (EPSILON * LN2) * combine(parts[...])


def call(kernel, name, outs, *args, scratch=(), inputs=None, cost=None, vmem=48):
    whole = pl.BlockSpec(memory_space=pltpu.VMEM)
    return pl.pallas_call(
        kernel,
        name=name,
        out_shape=[jax.ShapeDtypeStruct(*o) for o in outs],
        in_specs=[pl.BlockSpec(memory_space=space) for space in inputs or [pltpu.VMEM] * len(args)],
        out_specs=[whole] * len(outs),
        scratch_shapes=list(scratch),
        compiler_params=pltpu.CompilerParams(vmem_limit_bytes=vmem << 20),
        cost_estimate=cost,
    )(*args)


def exchange(v, axes):
    return lax.all_to_all(v, axes, 0, 0, tiled=True)


def swap(v, axis, offset):
    size = lax.axis_size(axis)
    return lax.ppermute(v, axis, [(i, i ^ offset) for i in range(size)])


def pinned(*arrays):
    return [pltpu.with_memory_space_constraint(v, pltpu.HBM) for v in arrays]


def local(src_points, log_a, tgt_points, log_b, g_init):
    own_s, own_t = src_points.shape[0], tgt_points.shape[0]
    across_t = lax.axis_size(TARGET_AXES)
    across_s = lax.axis_size(SOURCE_AXES)
    rows, cols = own_s * across_t, own_t * across_s
    row = lambda v: v.reshape(1, -1)
    spack, tpack, ssq, tsq = call(
        pack_kernel,
        "pack",
        [
            ((PACK, 2 * own_s), F32),
            ((across_s, 2 * DIM + 8, own_t // 2), F32),
            ((1, own_s), F32),
            ((1, own_t), F32),
        ],
        *pinned(src_points.T, row(log_a), tgt_points.T, row(log_b), row(g_init)),
        scratch=[pltpu.VMEM((DIM, own_s), F32), pltpu.VMEM((1, own_s), F32), pltpu.VMEM((DIM, own_t), F32)]
        + [pltpu.VMEM((1, own_t), F32)] * 2
        + [pltpu.SemaphoreType.DMA((5,))],
        inputs=[pltpu.HBM] * 5,
        vmem=8,
    )
    pair = call(
        join_kernel, "join", [((2 * PACK, 2 * own_s), F32)], spack, swap(spack, "z", 4), cost=JOIN_COST, vmem=2
    )[0]
    mine = jnp.concatenate([pair] + [swap(pair, "z", k) for k in (1, 2, 3)], axis=0)
    groups = [mine, swap(mine, "c", 1)]
    tpg = exchange(tpack, SOURCE_AXES)
    row_out = ((across_t, 8, rows // 8), F32)
    col_out = ((across_s, 8, cols // 8), F32)
    parts, akm, bkm, la, lb = call(
        first_kernel,
        "row_pass_first",
        [row_out, ((DEPTH, rows), BF16), ((DEPTH, cols), BF16), ((1, rows), F32), ((1, cols), F32)],
        *groups,
        *pinned(tpg),
        scratch=[pltpu.VMEM((cols, DEPTH), BF16), pltpu.VMEM((DEPTH, cols), BF16)]
        + [pltpu.VMEM((across_t, PACK, 2 * own_s), F32), pltpu.VMEM(tpg.shape, F32)]
        + [pltpu.SemaphoreType.DMA],
        inputs=[pltpu.VMEM] * 2 + [pltpu.HBM],
    )
    row_scratch = [pltpu.VMEM((cols, DEPTH), BF16), pltpu.VMEM((DEPTH, cols), BF16)]
    col_scratch = [pltpu.VMEM((rows, DEPTH), BF16), pltpu.VMEM((DEPTH, rows), BF16)]
    parts = exchange(parts, TARGET_AXES)
    (parts,) = call(column_kernel, "column_pass", [col_out], parts, la, akm, bkm, scratch=col_scratch)
    parts = exchange(parts, SOURCE_AXES)
    (parts,) = call(row_kernel, "row_pass", [row_out], parts, lb, akm, bkm, scratch=row_scratch)
    parts = exchange(parts, TARGET_AXES)
    parts, own_rows = call(
        last_column_kernel,
        "column_pass_last",
        [((across_s, 1, own_t), F32), ((1, own_s), F32)],
        parts,
        la,
        akm,
        bkm,
        scratch=col_scratch,
    )
    parts = exchange(parts, SOURCE_AXES)
    f, g = call(last_kernel, "last", [((1, own_s), F32), ((1, own_t), F32)], parts, own_rows, ssq, tsq)
    return f.reshape(own_s), g.reshape(own_t)


def solution(mesh):
    fine = Mesh(mesh.devices.reshape(4, 8, 4, 2), AXES)
    flat = P(AXES)
    return jax.shard_map(
        local,
        mesh=fine,
        in_specs=(P(AXES, None), flat, P(AXES, None), flat, flat),
        out_specs=(flat, flat),
        check_vma=False,
    )
```

profile of v0, /device:TPU:1, one launch (start us, length us, event | category | flops | bytes accessed | tf_op | source)
XLA Modules:
  0.0 94.3 jit_solution(1259979088578414777)
XLA Ops:
  0.6 1.7 %pack.1 = (f32[24,128]{1,0:T(8,128)S(1)}, f32[16,72,128]{2,1,0:T(8,128)}, f32[1,64]{1,0:T(1,128)S(1)}, f32[1,256]{1,0:T(1,128)S(1)}) custom-call(f32[32,64]{1,0:T(8,128)} %bitcast.8, f32[1,64]{1,0:T(1,128)} %bitcast.11, f32[32,256]{1,0:T(8,128)} %bitcast.7, f32[1,256]{1,0:T(1,128)} %bitcast.9, f32[1,256]{1,0:T(1,128)} %bitcast.10), custom_call_target="tpu_custom_call" | custom-call | tf_op jit(solution)/shard_map/pack/pallas_call | solution.py:224
  2.3 7.8 %collective-permute-start = (f32[24,128]{1,0:T(8,128)S(1)}, f32[24,128]{1,0:T(8,128)S(1)}, u32[]{:S(2)}, u32[]{:S(2)}) collective-permute-start(f32[24,128]{1,0:T(8,128)S(1)} %get-tuple-element.15.first), channel_id=1, source_target_pairs={{0,32},{8,40},{16,48},{24,56},{32,0},{40,8},{48,16},{56,24},{1,33}... | collective-permute-start | bytes 36872 | tf_op jit(solution)/shard_map/ppermute | solution.py:242
  10.2 6.8 %all-to-all-start = ((f32[16,72,128]{2,1,0:T(8,128)}), f32[16,72,128]{2,1,0:T(8,128)}, u32[]{:S(2)}, u32[]{:S(2)}) async-start(f32[16,72,128]{2,1,0:T(8,128)} %get-tuple-element.16), calls=%async_computation | async-start | bytes 1179648 | tf_op jit(solution)/shard_map/all_to_all | solution.py:237
  17.0 0.0 collective-permute-done.second
  17.0 1.7 %collective-permute-start.3 = (f32[48,128]{1,0:T(8,128)S(1)}, f32[48,128]{1,0:T(8,128)S(1)}, u32[]{:S(2)}, u32[]{:S(2)}) collective-permute-start(f32[48,128]{1,0:T(8,128)S(1)} %join.1), channel_id=1, source_target_pairs={{0,24},{8,16},{16,8},{24,0},{32,56},{40,48},{48,40},{56,32},{1,25}... | collective-permute-start | bytes 73736 | tf_op jit(solution)/shard_map/ppermute | solution.py:242
  18.7 0.3 collective-permute-start.2
  19.0 1.6 %collective-permute-start.1 = (f32[48,128]{1,0:T(8,128)S(1)}, f32[48,128]{1,0:T(8,128)S(1)}, u32[]{:S(2)}, u32[]{:S(2)}) collective-permute-start(f32[48,128]{1,0:T(8,128)S(1)} %join.1), channel_id=1, source_target_pairs={{0,8},{8,0},{16,24},{24,16},{32,40},{40,32},{48,56},{56,48},{1,9},... | collective-permute-start | bytes 73736 | tf_op jit(solution)/shard_map/ppermute | solution.py:242
  20.6 0.9 collective-permute-done.3
  21.6 1.2 %collective-permute-done.2 = f32[48,128]{1,0:T(8,128)S(1)} collective-permute-done((f32[48,128]{1,0:T(8,128)S(1)}, f32[48,128]{1,0:T(8,128)S(1)}, u32[]{:S(2)}, u32[]{:S(2)}) %collective-permute-start.2) | collective-permute-done | bytes 24608 | tf_op jit(solution)/shard_map/ppermute | solution.py:242
  22.8 0.0 collective-permute-done.1
  22.8 2.3 %collective-permute-start.4 = (f32[192,128]{1,0:T(8,128)S(1)}, f32[192,128]{1,0:T(8,128)S(1)}, u32[]{:S(2)}, u32[]{:S(2)}) collective-permute-start(f32[192,128]{1,0:T(8,128)S(1)} %pad_maximum_fusion.mine), channel_id=1, source_target_pairs={{0,1},{1,0},{2,3},{3,2},{4,5},{5,4},{6,7},{7,6},{8,9},{9,8},{10,11... | collective-permute-start | bytes 294920 | tf_op jit(solution)/shard_map/ppermute | solution.py:242
  25.1 0.9 %collective-permute-done.4.other = f32[192,128]{1,0:T(8,128)S(1)} collective-permute-done((f32[192,128]{1,0:T(8,128)S(1)}, f32[192,128]{1,0:T(8,128)S(1)}, u32[]{:S(2)}, u32[]{:S(2)}) %collective-permute-start.4) | collective-permute-done | bytes 98336 | tf_op jit(solution)/shard_map/ppermute | solution.py:242
  26.0 2.1 %all-to-all-done.tpg_hbm = f32[16,72,128]{2,1,0:T(8,128)} async-done(((f32[16,72,128]{2,1,0:T(8,128)}), f32[16,72,128]{2,1,0:T(8,128)}, u32[]{:S(2)}, u32[]{:S(2)}) %all-to-all-start) | async-done | bytes 589856 | tf_op jit(solution)/shard_map/all_to_all | solution.py:237
  28.1 4.0 %row_pass_first.1 = (f32[16,8,128]{2,1,0:T(8,128)S(1)}, bf16[128,1024]{1,0:T(8,128)(2,1)S(1)}, bf16[128,4096]{1,0:T(8,128)(2,1)S(1)}, f32[1,1024]{1,0:T(1,128)S(1)}, f32[1,4096]{1,0:T(1,128)S(1)}) custom-call(f32[192,128]{1,0:T(8,128)S(1)} %pad_maximum_fusion.mine, f32[192,128]{1,0:T(8,128)S(1)} %collective-permute-done.4.other, ...), custom_call_target="tpu_custom_call" | custom-call | tf_op jit(solution)/shard_map/row_pass_first/pallas_call | solution.py:224
  32.1 12.3 %all_to_all.25.parts = f32[16,8,128]{2,1,0:T(8,128)S(1)} all-to-all(f32[16,8,128]{2,1,0:T(8,128)S(1)} %get-tuple-element.17), channel_id=1, replica_groups=mesh['x'=4,'z'=8,'y'=4,'c'=2] {'c','z'}, dimensions={0} | all-to-all | bytes 131072 | tf_op jit(solution)/shard_map/all_to_all | solution.py:237
  44.4 2.7 %column_pass.1 = f32[16,8,512]{2,1,0:T(8,128)S(1)} custom-call(f32[16,8,128]{2,1,0:T(8,128)S(1)} %all_to_all.25.parts, f32[1,1024]{1,0:T(1,128)S(1)} %get-tuple-element.18.la, bf16[128,1024]{1,0:T(8,128)(2,1)S(1)} %get-tuple-element.19.akm, bf16[128,4096]{1,0:T(8,128)(2,1)S(1)} %get-tuple-element.20.bkm), custom_call_target="tpu_custom_call" | custom-call | tf_op jit(solution)/shard_map/column_pass/pallas_call | solution.py:224
  47.2 15.6 %all_to_all.26.parts = f32[16,8,512]{2,1,0:T(8,128)S(1)} all-to-all(f32[16,8,512]{2,1,0:T(8,128)S(1)} %column_pass.1), channel_id=1, replica_groups=mesh['x'=4,'z'=8,'y'=4,'c'=2] {'y','x'}, dimensions={0} | all-to-all | bytes 524288 | tf_op jit(solution)/shard_map/all_to_all | solution.py:237
  62.7 2.9 %row_pass.1 = f32[16,8,128]{2,1,0:T(8,128)S(1)} custom-call(f32[16,8,512]{2,1,0:T(8,128)S(1)} %all_to_all.26.parts, f32[1,4096]{1,0:T(1,128)S(1)} %get-tuple-element.21.lb, bf16[128,1024]{1,0:T(8,128)(2,1)S(1)} %get-tuple-element.19.akm, bf16[128,4096]{1,0:T(8,128)(2,1)S(1)} %get-tuple-element.20.bkm), custom_call_target="tpu_custom_call" | custom-call | tf_op jit(solution)/shard_map/row_pass/pallas_call | solution.py:224
  65.6 11.0 %all_to_all.27.parts = f32[16,8,128]{2,1,0:T(8,128)S(1)} all-to-all(f32[16,8,128]{2,1,0:T(8,128)S(1)} %row_pass.1), channel_id=1, replica_groups=mesh['x'=4,'z'=8,'y'=4,'c'=2] {'c','z'}, dimensions={0} | all-to-all | bytes 131072 | tf_op jit(solution)/shard_map/all_to_all | solution.py:237
  76.6 2.7 %column_pass_last.1 = (f32[16,1,256]{2,1,0:T(1,128)S(1)}, f32[1,64]{1,0:T(1,128)S(1)}) custom-call(f32[16,8,128]{2,1,0:T(8,128)S(1)} %all_to_all.27.parts, f32[1,1024]{1,0:T(1,128)S(1)} %get-tuple-element.18.la, bf16[128,1024]{1,0:T(8,128)(2,1)S(1)} %get-tuple-element.19.akm, bf16[128,4096]{1,0:T(8,128)(2,1)S(1)} %get-tuple-element.20.bkm), custom_call_target="tpu_custom_call" | custom-call | tf_op jit(solution)/shard_map/column_pass_last/pallas_call | solution.py:224
  79.2 14.4 %all_to_all.28.parts = f32[16,1,256]{2,1,0:T(1,128)S(1)} all-to-all(f32[16,1,256]{2,1,0:T(1,128)S(1)} %get-tuple-element.22), channel_id=1, replica_groups=mesh['x'=4,'z'=8,'y'=4,'c'=2] {'y','x'}, dimensions={0} | all-to-all | bytes 32768 | tf_op jit(solution)/shard_map/all_to_all | solution.py:237
  93.7 0.6 last.1
  (2 shorter events, 0.0 us)
Async XLA Ops:
  2.3 14.6 %collective-permute-start = (f32[24,128]{1,0:T(8,128)S(1)}, f32[24,128]{1,0:T(8,128)S(1)}, u32[]{:S(2)}, u32[]{:S(2)}) collective-permute-start(f32[24,128]{1,0:T(8,128)S(1)} %get-tuple-element.15.first), channel_id=1, source_target_pairs={{0,32},{8,40},{16,48},{24,56},{32,0},{40,8},{48,16},{56,24},{1,33}... | collective-permute-start | bytes 36872 | tf_op jit(solution)/shard_map/ppermute | solution.py:242
  10.2 17.9 %all-to-all-start = ((f32[16,72,128]{2,1,0:T(8,128)}), f32[16,72,128]{2,1,0:T(8,128)}, u32[]{:S(2)}, u32[]{:S(2)}) async-start(f32[16,72,128]{2,1,0:T(8,128)} %get-tuple-element.16), calls=%async_computation | async-start | bytes 1179648 | tf_op jit(solution)/shard_map/all_to_all | solution.py:237
  17.0 4.6 %collective-permute-start.3 = (f32[48,128]{1,0:T(8,128)S(1)}, f32[48,128]{1,0:T(8,128)S(1)}, u32[]{:S(2)}, u32[]{:S(2)}) collective-permute-start(f32[48,128]{1,0:T(8,128)S(1)} %join.1), channel_id=1, source_target_pairs={{0,24},{8,16},{16,8},{24,0},{32,56},{40,48},{48,40},{56,32},{1,25}... | collective-permute-start | bytes 73736 | tf_op jit(solution)/shard_map/ppermute | solution.py:242
  18.7 4.0 %collective-permute-start.2 = (f32[48,128]{1,0:T(8,128)S(1)}, f32[48,128]{1,0:T(8,128)S(1)}, u32[]{:S(2)}, u32[]{:S(2)}) collective-permute-start(f32[48,128]{1,0:T(8,128)S(1)} %join.1), channel_id=1, source_target_pairs={{0,16},{8,24},{16,0},{24,8},{32,48},{40,56},{48,32},{56,40},{1,17}... | collective-permute-start | bytes 73736 | tf_op jit(solution)/shard_map/ppermute | solution.py:242
  19.0 3.8 %collective-permute-start.1 = (f32[48,128]{1,0:T(8,128)S(1)}, f32[48,128]{1,0:T(8,128)S(1)}, u32[]{:S(2)}, u32[]{:S(2)}) collective-permute-start(f32[48,128]{1,0:T(8,128)S(1)} %join.1), channel_id=1, source_target_pairs={{0,8},{8,0},{16,24},{24,16},{32,40},{40,32},{48,56},{56,48},{1,9},... | collective-permute-start | bytes 73736 | tf_op jit(solution)/shard_map/ppermute | solution.py:242
  22.8 3.2 %collective-permute-start.4 = (f32[192,128]{1,0:T(8,128)S(1)}, f32[192,128]{1,0:T(8,128)S(1)}, u32[]{:S(2)}, u32[]{:S(2)}) collective-permute-start(f32[192,128]{1,0:T(8,128)S(1)} %pad_maximum_fusion.mine), channel_id=1, source_target_pairs={{0,1},{1,0},{2,3},{3,2},{4,5},{5,4},{6,7},{7,6},{8,9},{9,8},{10,11... | collective-permute-start | bytes 294920 | tf_op jit(solution)/shard_map/ppermute | solution.py:242
where the time goes:
time: 94.9 us; the launch traced here: 94.3 us
  blocking collectives  53.3 us (56%)
  starting transfers between devices  20.5 us (22%)
  Pallas kernels  14.6 us (15%)
  waiting for transfers between devices  5.18 us (5%)
    all_to_all x4, blocking collectives, exchange(): return lax.all_to_all(v, axes, 0, 0, tiled=True)  53.3 us
    pallas_call x7, Pallas kernels, call(): pl.pallas_call(kernel, name=name, out_shape=[jax.ShapeDtypeStruct(*o) for...  14.6 us
    ppermute x5, starting transfers between devices, swap(): return lax.ppermute(v, axis, [(i, i ^ offset) for i in range(size)])  13.7 us
    all_to_all x1, starting transfers between devices, exchange(): return lax.all_to_all(v, axes, 0, 0, tiled=True)  6.8 us
    ppermute x5, waiting for transfers between devices, swap(): return lax.ppermute(v, axis, [(i, i ^ offset) for i in range(size)])  3.1 us
    all_to_all x1, waiting for transfers between devices, exchange(): return lax.all_to_all(v, axes, 0, 0, tiled=True)  2.09 us
  transfers between devices with their start and end apart: 6, of which 4 were waited for; matrix products, arithmetic and copies ran while one was open for 0% of the time, Pallas kernels for 0%

commit v1 on v0

--- a/solution.py
+++ b/solution.py
@@ -10,9 +10,10 @@
 EPSILON = 0.5
 LOG2E = float(np.log2(np.e))
 LN2 = float(np.log(2.0))
-AXES = ("x", "z", "y", "c")
+Z = ("z2", "z1", "z0")
+AXES = ("x", *Z, "y", "c")
 SOURCE_AXES = ("y", "x")
-TARGET_AXES = ("c", "z")
+TARGET_AXES = ("c", "z1", "z2", "z0")
 DIM = 32
 PACK = DIM // 2 + 8
 DEPTH = 128
@@ -22,7 +23,7 @@
 OVERFLOW = 1e38
 F32 = jnp.float32
 BF16 = jnp.bfloat16
-Z_ORDER = (0, 4, 1, 5, 2, 6, 3, 7)
+Z_ORDER = (0, 2, 1, 3, 4, 6, 5, 7)
 JOIN_COST = pl.CostEstimate(flops=1000000000000, bytes_accessed=0, transcendentals=0)
 
 
@@ -269,9 +270,9 @@
         vmem=8,
     )
     pair = call(
-        join_kernel, "join", [((2 * PACK, 2 * own_s), F32)], spack, swap(spack, "z", 4), cost=JOIN_COST, vmem=2
+        join_kernel, "join", [((2 * PACK, 2 * own_s), F32)], spack, swap(spack, Z, 4), cost=JOIN_COST, vmem=2
     )[0]
-    mine = jnp.concatenate([pair] + [swap(pair, "z", k) for k in (1, 2, 3)], axis=0)
+    mine = jnp.concatenate([pair] + [swap(pair, Z, k) for k in (1, 2, 3)], axis=0)
     groups = [mine, swap(mine, "c", 1)]
     tpg = exchange(tpack, SOURCE_AXES)
     row_out = ((across_t, 8, rows // 8), F32)
@@ -310,7 +311,7 @@
 
 
 def solution(mesh):
-    fine = Mesh(mesh.devices.reshape(4, 8, 4, 2), AXES)
+    fine = Mesh(mesh.devices.reshape(4, 2, 2, 2, 4, 2), AXES)
     flat = P(AXES)
     return jax.shard_map(
         local,

time: 94.9 us -> 96.8 us (1.020)
  the two profiles are of different devices: /device:TPU:1 before, /device:TPU:2 now
where the time goes in v1:
time: 96.8 us; the launch traced here: 96.5 us
  blocking collectives  43.4 us (45%)
  Pallas kernels  27 us (28%)
  starting transfers between devices  19.3 us (20%)
  waiting for transfers between devices  6.09 us (6%)
    all_to_all x4, blocking collectives, exchange(): return lax.all_to_all(v, axes, 0, 0, tiled=True)  43.4 us
    pallas_call x7, Pallas kernels, call(): pl.pallas_call(kernel, name=name, out_shape=[jax.ShapeDtypeStruct(*o) for...  27 us
    ppermute x5, starting transfers between devices, swap(): return lax.ppermute(v, axis, [(i, i ^ offset) for i in range(size)])  11.8 us
    all_to_all x1, starting transfers between devices, exchange(): return lax.all_to_all(v, axes, 0, 0, tiled=True)  7.48 us
    ppermute x5, waiting for transfers between devices, swap(): return lax.ppermute(v, axis, [(i, i ^ offset) for i in range(size)])  3.56 us
    all_to_all x1, waiting for transfers between devices, exchange(): return lax.all_to_all(v, axes, 0, 0, tiled=True)  2.54 us
  transfers between devices with their start and end apart: 6, of which 4 were waited for; matrix products, arithmetic and copies ran while one was open for 0% of the time, Pallas kernels for 0%

profile of v1, /device:TPU:2, one launch (start us, length us, event | category | flops | bytes accessed | tf_op | source)
XLA Modules:
  0.0 96.5 jit_solution(13820252391969905410)
XLA Ops:
  0.6 1.7 %pack.1 = (f32[24,128]{1,0:T(8,128)S(1)}, f32[16,72,128]{2,1,0:T(8,128)}, f32[1,64]{1,0:T(1,128)S(1)}, f32[1,256]{1,0:T(1,128)S(1)}) custom-call(f32[32,64]{1,0:T(8,128)} %bitcast.8, f32[1,64]{1,0:T(1,128)} %bitcast.11, f32[32,256]{1,0:T(8,128)} %bitcast.7, f32[1,256]{1,0:T(1,128)} %bitcast.9, f32[1,256]{1,0:T(1,128)} %bitcast.10), custom_call_target="tpu_custom_call" | custom-call | tf_op jit(solution)/shard_map/pack/pallas_call | solution.py:225
  2.3 7.3 %collective-permute-start = (f32[24,128]{1,0:T(8,128)S(1)}, f32[24,128]{1,0:T(8,128)S(1)}, u32[]{:S(2)}, u32[]{:S(2)}) collective-permute-start(f32[24,128]{1,0:T(8,128)S(1)} %get-tuple-element.15.first), channel_id=1, source_target_pairs={{0,32},{8,40},{16,48},{24,56},{32,0},{40,8},{48,16},{56,24},{1,33}... | collective-permute-start | bytes 36872 | tf_op jit(solution)/shard_map/ppermute | solution.py:243
  9.6 7.5 %all-to-all-start = ((f32[16,72,128]{2,1,0:T(8,128)}), f32[16,72,128]{2,1,0:T(8,128)}, u32[]{:S(2)}, u32[]{:S(2)}) async-start(f32[16,72,128]{2,1,0:T(8,128)} %get-tuple-element.16), calls=%async_computation | async-start | bytes 1179648 | tf_op jit(solution)/shard_map/all_to_all | solution.py:238
  17.1 0.0 collective-permute-done.second
  17.1 2.0 %collective-permute-start.3 = (f32[48,128]{1,0:T(8,128)S(1)}, f32[48,128]{1,0:T(8,128)S(1)}, u32[]{:S(2)}, u32[]{:S(2)}) collective-permute-start(f32[48,128]{1,0:T(8,128)S(1)} %join.1), channel_id=1, source_target_pairs={{0,24},{8,16},{16,8},{24,0},{32,56},{40,48},{48,40},{56,32},{1,25}... | collective-permute-start | bytes 73736 | tf_op jit(solution)/shard_map/ppermute | solution.py:243
  19.1 0.6 collective-permute-start.2
  19.7 1.9 %collective-permute-start.1 = (f32[48,128]{1,0:T(8,128)S(1)}, f32[48,128]{1,0:T(8,128)S(1)}, u32[]{:S(2)}, u32[]{:S(2)}) collective-permute-start(f32[48,128]{1,0:T(8,128)S(1)} %join.1), channel_id=1, source_target_pairs={{0,8},{8,0},{16,24},{24,16},{32,40},{40,32},{48,56},{56,48},{1,9},... | collective-permute-start | bytes 73736 | tf_op jit(solution)/shard_map/ppermute | solution.py:243
  21.6 1.5 %collective-permute-done.3 = f32[48,128]{1,0:T(8,128)S(1)} collective-permute-done((f32[48,128]{1,0:T(8,128)S(1)}, f32[48,128]{1,0:T(8,128)S(1)}, u32[]{:S(2)}, u32[]{:S(2)}) %collective-permute-start.3) | collective-permute-done | bytes 24608 | tf_op jit(solution)/shard_map/ppermute | solution.py:243
  23.0 0.8 collective-permute-done.2
  23.9 0.0 collective-permute-done.1
  23.9 0.1 collective-permute-start.4
  24.0 1.3 %collective-permute-done.4.other = f32[192,128]{1,0:T(8,128)S(1)} collective-permute-done((f32[192,128]{1,0:T(8,128)S(1)}, f32[192,128]{1,0:T(8,128)S(1)}, u32[]{:S(2)}, u32[]{:S(2)}) %collective-permute-start.4) | collective-permute-done | bytes 98336 | tf_op jit(solution)/shard_map/ppermute | solution.py:243
  25.3 2.5 %all-to-all-done.tpg_hbm = f32[16,72,128]{2,1,0:T(8,128)} async-done(((f32[16,72,128]{2,1,0:T(8,128)}), f32[16,72,128]{2,1,0:T(8,128)}, u32[]{:S(2)}, u32[]{:S(2)}) %all-to-all-start) | async-done | bytes 589856 | tf_op jit(solution)/shard_map/all_to_all | solution.py:238
  27.8 4.0 %row_pass_first.1 = (f32[16,8,128]{2,1,0:T(8,128)S(1)}, bf16[128,1024]{1,0:T(8,128)(2,1)S(1)}, bf16[128,4096]{1,0:T(8,128)(2,1)S(1)}, f32[1,1024]{1,0:T(1,128)S(1)}, f32[1,4096]{1,0:T(1,128)S(1)}) custom-call(f32[192,128]{1,0:T(8,128)S(1)} %pad_maximum_fusion.mine, f32[192,128]{1,0:T(8,128)S(1)} %collective-permute-done.4.other, ...), custom_call_target="tpu_custom_call" | custom-call | tf_op jit(solution)/shard_map/row_pass_first/pallas_call | solution.py:225
  31.8 11.0 %all_to_all.25.parts = f32[16,8,128]{2,1,0:T(8,128)S(1)} all-to-all(f32[16,8,128]{2,1,0:T(8,128)S(1)} %get-tuple-element.17), channel_id=1, replica_groups=mesh['x'=4,'z2'=2,'z1'=2,'z0'=2,'y'=4,'c'=2] {'c','z1','z2','z0'}, dimensions={0} | all-to-all | bytes 131072 | tf_op jit(solution)/shard_map/all_to_all | solution.py:238
  42.8 9.0 %column_pass.1 = f32[16,8,512]{2,1,0:T(8,128)S(1)} custom-call(f32[16,8,128]{2,1,0:T(8,128)S(1)} %all_to_all.25.parts, f32[1,1024]{1,0:T(1,128)S(1)} %get-tuple-element.18.la, bf16[128,1024]{1,0:T(8,128)(2,1)S(1)} %get-tuple-element.19.akm, bf16[128,4096]{1,0:T(8,128)(2,1)S(1)} %get-tuple-element.20.bkm), custom_call_target="tpu_custom_call" | custom-call | tf_op jit(solution)/shard_map/column_pass/pallas_call | solution.py:225
  51.8 11.6 %all_to_all.26.parts = f32[16,8,512]{2,1,0:T(8,128)S(1)} all-to-all(f32[16,8,512]{2,1,0:T(8,128)S(1)} %column_pass.1), channel_id=1, replica_groups=mesh['x'=4,'z2'=2,'z1'=2,'z0'=2,'y'=4,'c'=2] {'y','x'}, dimensions={0} | all-to-all | bytes 524288 | tf_op jit(solution)/shard_map/all_to_all | solution.py:238
  63.4 2.9 %row_pass.1 = f32[16,8,128]{2,1,0:T(8,128)S(1)} custom-call(f32[16,8,512]{2,1,0:T(8,128)S(1)} %all_to_all.26.parts, f32[1,4096]{1,0:T(1,128)S(1)} %get-tuple-element.21.lb, bf16[128,1024]{1,0:T(8,128)(2,1)S(1)} %get-tuple-element.19.akm, bf16[128,4096]{1,0:T(8,128)(2,1)S(1)} %get-tuple-element.20.bkm), custom_call_target="tpu_custom_call" | custom-call | tf_op jit(solution)/shard_map/row_pass/pallas_call | solution.py:225
  66.3 10.4 %all_to_all.27.parts = f32[16,8,128]{2,1,0:T(8,128)S(1)} all-to-all(f32[16,8,128]{2,1,0:T(8,128)S(1)} %row_pass.1), channel_id=1, replica_groups=mesh['x'=4,'z2'=2,'z1'=2,'z0'=2,'y'=4,'c'=2] {'c','z1','z2','z0'}, dimensions={0} | all-to-all | bytes 131072 | tf_op jit(solution)/shard_map/all_to_all | solution.py:238
  76.7 8.8 %column_pass_last.1 = (f32[16,1,256]{2,1,0:T(1,128)S(1)}, f32[1,64]{1,0:T(1,128)S(1)}) custom-call(f32[16,8,128]{2,1,0:T(8,128)S(1)} %all_to_all.27.parts, f32[1,1024]{1,0:T(1,128)S(1)} %get-tuple-element.18.la, bf16[128,1024]{1,0:T(8,128)(2,1)S(1)} %get-tuple-element.19.akm, bf16[128,4096]{1,0:T(8,128)(2,1)S(1)} %get-tuple-element.20.bkm), custom_call_target="tpu_custom_call" | custom-call | tf_op jit(solution)/shard_map/column_pass_last/pallas_call | solution.py:225
  85.6 10.3 %all_to_all.28.parts = f32[16,1,256]{2,1,0:T(1,128)S(1)} all-to-all(f32[16,1,256]{2,1,0:T(1,128)S(1)} %get-tuple-element.22), channel_id=1, replica_groups=mesh['x'=4,'z2'=2,'z1'=2,'z0'=2,'y'=4,'c'=2] {'y','x'}, dimensions={0} | all-to-all | bytes 32768 | tf_op jit(solution)/shard_map/all_to_all | solution.py:238
  95.9 0.6 last.1
  (2 shorter events, 0.0 us)
Async XLA Ops:
  2.3 14.8 %collective-permute-start = (f32[24,128]{1,0:T(8,128)S(1)}, f32[24,128]{1,0:T(8,128)S(1)}, u32[]{:S(2)}, u32[]{:S(2)}) collective-permute-start(f32[24,128]{1,0:T(8,128)S(1)} %get-tuple-element.15.first), channel_id=1, source_target_pairs={{0,32},{8,40},{16,48},{24,56},{32,0},{40,8},{48,16},{56,24},{1,33}... | collective-permute-start | bytes 36872 | tf_op jit(solution)/shard_map/ppermute | solution.py:243
  9.6 18.2 %all-to-all-start = ((f32[16,72,128]{2,1,0:T(8,128)}), f32[16,72,128]{2,1,0:T(8,128)}, u32[]{:S(2)}, u32[]{:S(2)}) async-start(f32[16,72,128]{2,1,0:T(8,128)} %get-tuple-element.16), calls=%async_computation | async-start | bytes 1179648 | tf_op jit(solution)/shard_map/all_to_all | solution.py:238
  17.1 5.9 %collective-permute-start.3 = (f32[48,128]{1,0:T(8,128)S(1)}, f32[48,128]{1,0:T(8,128)S(1)}, u32[]{:S(2)}, u32[]{:S(2)}) collective-permute-start(f32[48,128]{1,0:T(8,128)S(1)} %join.1), channel_id=1, source_target_pairs={{0,24},{8,16},{16,8},{24,0},{32,56},{40,48},{48,40},{56,32},{1,25}... | collective-permute-start | bytes 73736 | tf_op jit(solution)/shard_map/ppermute | solution.py:243
  19.1 4.7 %collective-permute-start.2 = (f32[48,128]{1,0:T(8,128)S(1)}, f32[48,128]{1,0:T(8,128)S(1)}, u32[]{:S(2)}, u32[]{:S(2)}) collective-permute-start(f32[48,128]{1,0:T(8,128)S(1)} %join.1), channel_id=1, source_target_pairs={{0,16},{8,24},{16,0},{24,8},{32,48},{40,56},{48,32},{56,40},{1,17}... | collective-permute-start | bytes 73736 | tf_op jit(solution)/shard_map/ppermute | solution.py:243
  19.7 4.2 %collective-permute-start.1 = (f32[48,128]{1,0:T(8,128)S(1)}, f32[48,128]{1,0:T(8,128)S(1)}, u32[]{:S(2)}, u32[]{:S(2)}) collective-permute-start(f32[48,128]{1,0:T(8,128)S(1)} %join.1), channel_id=1, source_target_pairs={{0,8},{8,0},{16,24},{24,16},{32,40},{40,32},{48,56},{56,48},{1,9},... | collective-permute-start | bytes 73736 | tf_op jit(solution)/shard_map/ppermute | solution.py:243
  23.9 1.4 %collective-permute-start.4 = (f32[192,128]{1,0:T(8,128)S(1)}, f32[192,128]{1,0:T(8,128)S(1)}, u32[]{:S(2)}, u32[]{:S(2)}) collective-permute-start(f32[192,128]{1,0:T(8,128)S(1)} %pad_maximum_fusion.mine), channel_id=1, source_target_pairs={{0,1},{1,0},{2,3},{3,2},{4,5},{5,4},{6,7},{7,6},{8,9},{9,8},{10,11... | collective-permute-start | bytes 294920 | tf_op jit(solution)/shard_map/ppermute | solution.py:243

commit v2 on v0

--- a/solution.py
+++ b/solution.py
@@ -59,13 +59,14 @@
     for at in range(0, rhs_ref.shape[1], TILE):
         rhs = rhs_ref[:, at : at + TILE]
         top = total = None
-        for row in range(0, lhs_ref.shape[0], CHUNK):
+        size = CHUNK if at == 0 or lhs_ref.shape[0] < rhs_ref.shape[1] else CHUNK // 2
+        for row in range(0, lhs_ref.shape[0], size):
             if at == 0:
                 lhs = lhs_t[:, row : row + CHUNK].T
                 lhs_ref[row : row + CHUNK, :] = lhs
             else:
-                lhs = lhs_ref[row : row + CHUNK, :]
-            terms = jnp.dot(lhs, rhs, preferred_element_type=F32).reshape(CHUNK // 8, 8, TILE)
+                lhs = lhs_ref[row : row + size, :]
+            terms = jnp.dot(lhs, rhs, preferred_element_type=F32).reshape(size // 8, 8, TILE)
             if top is None:
                 top = jnp.max(jnp.max(terms, axis=0), axis=0, keepdims=True)
             added = jnp.sum(jnp.exp2(terms - top[None]), axis=0)

time: 94.9 us -> 97 us (1.022)
  the two profiles are of different devices: /device:TPU:1 before, /device:TPU:32 now
where the time goes in v2:
time: 97 us; the launch traced here: 96.6 us
  blocking collectives  55.9 us (58%)
  starting transfers between devices  17.1 us (18%)
  Pallas kernels  14.5 us (15%)
  waiting for transfers between devices  8.31 us (9%)
    all_to_all x4, blocking collectives, exchange(): return lax.all_to_all(v, axes, 0, 0, tiled=True)  55.9 us
    pallas_call x7, Pallas kernels, call(): pl.pallas_call(kernel, name=name, out_shape=[jax.ShapeDtypeStruct(*o) for...  14.5 us
    ppermute x5, starting transfers between devices, swap(): return lax.ppermute(v, axis, [(i, i ^ offset) for i in range(size)])  10 us
    all_to_all x1, starting transfers between devices, exchange(): return lax.all_to_all(v, axes, 0, 0, tiled=True)  7.08 us
    ppermute x5, waiting for transfers between devices, swap(): return lax.ppermute(v, axis, [(i, i ^ offset) for i in range(size)])  5 us
    all_to_all x1, waiting for transfers between devices, exchange(): return lax.all_to_all(v, axes, 0, 0, tiled=True)  3.31 us
  transfers between devices with their start and end apart: 6, of which 5 were waited for; matrix products, arithmetic and copies ran while one was open for 0% of the time, Pallas kernels for 0%

profile of v2, /device:TPU:32, one launch (start us, length us, event | category | flops | bytes accessed | tf_op | source)
XLA Modules:
  0.0 96.6 jit_solution(11795904000615809726)
XLA Ops:
  0.6 1.7 %pack.1 = (f32[24,128]{1,0:T(8,128)S(1)}, f32[16,72,128]{2,1,0:T(8,128)}, f32[1,64]{1,0:T(1,128)S(1)}, f32[1,256]{1,0:T(1,128)S(1)}) custom-call(f32[32,64]{1,0:T(8,128)} %bitcast.8, f32[1,64]{1,0:T(1,128)} %bitcast.11, f32[32,256]{1,0:T(8,128)} %bitcast.7, f32[1,256]{1,0:T(1,128)} %bitcast.9, f32[1,256]{1,0:T(1,128)} %bitcast.10), custom_call_target="tpu_custom_call" | custom-call | tf_op jit(solution)/shard_map/pack/pallas_call | solution.py:225
  2.3 6.4 %collective-permute-start = (f32[24,128]{1,0:T(8,128)S(1)}, f32[24,128]{1,0:T(8,128)S(1)}, u32[]{:S(2)}, u32[]{:S(2)}) collective-permute-start(f32[24,128]{1,0:T(8,128)S(1)} %get-tuple-element.15.first), channel_id=1, source_target_pairs={{0,32},{8,40},{16,48},{24,56},{32,0},{40,8},{48,16},{56,24},{1,33}... | collective-permute-start | bytes 36872 | tf_op jit(solution)/shard_map/ppermute | solution.py:243
  8.7 7.1 %all-to-all-start = ((f32[16,72,128]{2,1,0:T(8,128)}), f32[16,72,128]{2,1,0:T(8,128)}, u32[]{:S(2)}, u32[]{:S(2)}) async-start(f32[16,72,128]{2,1,0:T(8,128)} %get-tuple-element.16), calls=%async_computation | async-start | bytes 1179648 | tf_op jit(solution)/shard_map/all_to_all | solution.py:238
  15.8 0.0 collective-permute-done.second
  15.8 1.1 %collective-permute-start.3 = (f32[48,128]{1,0:T(8,128)S(1)}, f32[48,128]{1,0:T(8,128)S(1)}, u32[]{:S(2)}, u32[]{:S(2)}) collective-permute-start(f32[48,128]{1,0:T(8,128)S(1)} %join.1), channel_id=1, source_target_pairs={{0,24},{8,16},{16,8},{24,0},{32,56},{40,48},{48,40},{56,32},{1,25}... | collective-permute-start | bytes 73736 | tf_op jit(solution)/shard_map/ppermute | solution.py:243
  16.9 2.4 %collective-permute-start.2 = (f32[48,128]{1,0:T(8,128)S(1)}, f32[48,128]{1,0:T(8,128)S(1)}, u32[]{:S(2)}, u32[]{:S(2)}) collective-permute-start(f32[48,128]{1,0:T(8,128)S(1)} %join.1), channel_id=1, source_target_pairs={{0,16},{8,24},{16,0},{24,8},{32,48},{40,56},{48,32},{56,40},{1,17}... | collective-permute-start | bytes 73736 | tf_op jit(solution)/shard_map/ppermute | solution.py:243
  19.3 0.1 collective-permute-start.1
  19.4 0.6 collective-permute-done.3
  20.0 1.6 %collective-permute-done.2 = f32[48,128]{1,0:T(8,128)S(1)} collective-permute-done((f32[48,128]{1,0:T(8,128)S(1)}, f32[48,128]{1,0:T(8,128)S(1)}, u32[]{:S(2)}, u32[]{:S(2)}) %collective-permute-start.2) | collective-permute-done | bytes 24608 | tf_op jit(solution)/shard_map/ppermute | solution.py:243
  21.7 1.5 %collective-permute-done.1 = f32[48,128]{1,0:T(8,128)S(1)} collective-permute-done((f32[48,128]{1,0:T(8,128)S(1)}, f32[48,128]{1,0:T(8,128)S(1)}, u32[]{:S(2)}, u32[]{:S(2)}) %collective-permute-start.1) | collective-permute-done | bytes 24608 | tf_op jit(solution)/shard_map/ppermute | solution.py:243
  23.1 0.1 collective-permute-start.4
  23.2 1.3 %collective-permute-done.4.other = f32[192,128]{1,0:T(8,128)S(1)} collective-permute-done((f32[192,128]{1,0:T(8,128)S(1)}, f32[192,128]{1,0:T(8,128)S(1)}, u32[]{:S(2)}, u32[]{:S(2)}) %collective-permute-start.4) | collective-permute-done | bytes 98336 | tf_op jit(solution)/shard_map/ppermute | solution.py:243
  24.5 3.3 %all-to-all-done.tpg_hbm = f32[16,72,128]{2,1,0:T(8,128)} async-done(((f32[16,72,128]{2,1,0:T(8,128)}), f32[16,72,128]{2,1,0:T(8,128)}, u32[]{:S(2)}, u32[]{:S(2)}) %all-to-all-start) | async-done | bytes 589856 | tf_op jit(solution)/shard_map/all_to_all | solution.py:238
  27.8 4.0 %row_pass_first.1 = (f32[16,8,128]{2,1,0:T(8,128)S(1)}, bf16[128,1024]{1,0:T(8,128)(2,1)S(1)}, bf16[128,4096]{1,0:T(8,128)(2,1)S(1)}, f32[1,1024]{1,0:T(1,128)S(1)}, f32[1,4096]{1,0:T(1,128)S(1)}) custom-call(f32[192,128]{1,0:T(8,128)S(1)} %pad_maximum_fusion.mine, f32[192,128]{1,0:T(8,128)S(1)} %collective-permute-done.4.other, ...), custom_call_target="tpu_custom_call" | custom-call | tf_op jit(solution)/shard_map/row_pass_first/pallas_call | solution.py:225
  31.8 11.0 %all_to_all.25.parts = f32[16,8,128]{2,1,0:T(8,128)S(1)} all-to-all(f32[16,8,128]{2,1,0:T(8,128)S(1)} %get-tuple-element.17), channel_id=1, replica_groups=mesh['x'=4,'z'=8,'y'=4,'c'=2] {'c','z'}, dimensions={0} | all-to-all | bytes 131072 | tf_op jit(solution)/shard_map/all_to_all | solution.py:238
  42.8 2.7 %column_pass.1 = f32[16,8,512]{2,1,0:T(8,128)S(1)} custom-call(f32[16,8,128]{2,1,0:T(8,128)S(1)} %all_to_all.25.parts, f32[1,1024]{1,0:T(1,128)S(1)} %get-tuple-element.18.la, bf16[128,1024]{1,0:T(8,128)(2,1)S(1)} %get-tuple-element.19.akm, bf16[128,4096]{1,0:T(8,128)(2,1)S(1)} %get-tuple-element.20.bkm), custom_call_target="tpu_custom_call" | custom-call | tf_op jit(solution)/shard_map/column_pass/pallas_call | solution.py:225
  45.6 18.2 %all_to_all.26.parts = f32[16,8,512]{2,1,0:T(8,128)S(1)} all-to-all(f32[16,8,512]{2,1,0:T(8,128)S(1)} %column_pass.1), channel_id=1, replica_groups=mesh['x'=4,'z'=8,'y'=4,'c'=2] {'y','x'}, dimensions={0} | all-to-all | bytes 524288 | tf_op jit(solution)/shard_map/all_to_all | solution.py:238
  63.7 2.8 %row_pass.1 = f32[16,8,128]{2,1,0:T(8,128)S(1)} custom-call(f32[16,8,512]{2,1,0:T(8,128)S(1)} %all_to_all.26.parts, f32[1,4096]{1,0:T(1,128)S(1)} %get-tuple-element.21.lb, bf16[128,1024]{1,0:T(8,128)(2,1)S(1)} %get-tuple-element.19.akm, bf16[128,4096]{1,0:T(8,128)(2,1)S(1)} %get-tuple-element.20.bkm), custom_call_target="tpu_custom_call" | custom-call | tf_op jit(solution)/shard_map/row_pass/pallas_call | solution.py:225
  66.6 10.1 %all_to_all.27.parts = f32[16,8,128]{2,1,0:T(8,128)S(1)} all-to-all(f32[16,8,128]{2,1,0:T(8,128)S(1)} %row_pass.1), channel_id=1, replica_groups=mesh['x'=4,'z'=8,'y'=4,'c'=2] {'c','z'}, dimensions={0} | all-to-all | bytes 131072 | tf_op jit(solution)/shard_map/all_to_all | solution.py:238
  76.7 2.7 %column_pass_last.1 = (f32[16,1,256]{2,1,0:T(1,128)S(1)}, f32[1,64]{1,0:T(1,128)S(1)}) custom-call(f32[16,8,128]{2,1,0:T(8,128)S(1)} %all_to_all.27.parts, f32[1,1024]{1,0:T(1,128)S(1)} %get-tuple-element.18.la, bf16[128,1024]{1,0:T(8,128)(2,1)S(1)} %get-tuple-element.19.akm, bf16[128,4096]{1,0:T(8,128)(2,1)S(1)} %get-tuple-element.20.bkm), custom_call_target="tpu_custom_call" | custom-call | tf_op jit(solution)/shard_map/column_pass_last/pallas_call | solution.py:225
  79.3 16.6 %all_to_all.28.parts = f32[16,1,256]{2,1,0:T(1,128)S(1)} all-to-all(f32[16,1,256]{2,1,0:T(1,128)S(1)} %get-tuple-element.22), channel_id=1, replica_groups=mesh['x'=4,'z'=8,'y'=4,'c'=2] {'y','x'}, dimensions={0} | all-to-all | bytes 32768 | tf_op jit(solution)/shard_map/all_to_all | solution.py:238
  96.0 0.6 last.1
  (2 shorter events, 0.0 us)
Async XLA Ops:
  2.3 13.5 %collective-permute-start = (f32[24,128]{1,0:T(8,128)S(1)}, f32[24,128]{1,0:T(8,128)S(1)}, u32[]{:S(2)}, u32[]{:S(2)}) collective-permute-start(f32[24,128]{1,0:T(8,128)S(1)} %get-tuple-element.15.first), channel_id=1, source_target_pairs={{0,32},{8,40},{16,48},{24,56},{32,0},{40,8},{48,16},{56,24},{1,33}... | collective-permute-start | bytes 36872 | tf_op jit(solution)/shard_map/ppermute | solution.py:243
  8.7 19.1 %all-to-all-start = ((f32[16,72,128]{2,1,0:T(8,128)}), f32[16,72,128]{2,1,0:T(8,128)}, u32[]{:S(2)}, u32[]{:S(2)}) async-start(f32[16,72,128]{2,1,0:T(8,128)} %get-tuple-element.16), calls=%async_computation | async-start | bytes 1179648 | tf_op jit(solution)/shard_map/all_to_all | solution.py:238
  15.8 4.2 %collective-permute-start.3 = (f32[48,128]{1,0:T(8,128)S(1)}, f32[48,128]{1,0:T(8,128)S(1)}, u32[]{:S(2)}, u32[]{:S(2)}) collective-permute-start(f32[48,128]{1,0:T(8,128)S(1)} %join.1), channel_id=1, source_target_pairs={{0,24},{8,16},{16,8},{24,0},{32,56},{40,48},{48,40},{56,32},{1,25}... | collective-permute-start | bytes 73736 | tf_op jit(solution)/shard_map/ppermute | solution.py:243
  16.9 4.7 %collective-permute-start.2 = (f32[48,128]{1,0:T(8,128)S(1)}, f32[48,128]{1,0:T(8,128)S(1)}, u32[]{:S(2)}, u32[]{:S(2)}) collective-permute-start(f32[48,128]{1,0:T(8,128)S(1)} %join.1), channel_id=1, source_target_pairs={{0,16},{8,24},{16,0},{24,8},{32,48},{40,56},{48,32},{56,40},{1,17}... | collective-permute-start | bytes 73736 | tf_op jit(solution)/shard_map/ppermute | solution.py:243
  19.3 3.8 %collective-permute-start.1 = (f32[48,128]{1,0:T(8,128)S(1)}, f32[48,128]{1,0:T(8,128)S(1)}, u32[]{:S(2)}, u32[]{:S(2)}) collective-permute-start(f32[48,128]{1,0:T(8,128)S(1)} %join.1), channel_id=1, source_target_pairs={{0,8},{8,0},{16,24},{24,16},{32,40},{40,32},{48,56},{56,48},{1,9},... | collective-permute-start | bytes 73736 | tf_op jit(solution)/shard_map/ppermute | solution.py:243
  23.1 1.4 %collective-permute-start.4 = (f32[192,128]{1,0:T(8,128)S(1)}, f32[192,128]{1,0:T(8,128)S(1)}, u32[]{:S(2)}, u32[]{:S(2)}) collective-permute-start(f32[192,128]{1,0:T(8,128)S(1)} %pad_maximum_fusion.mine), channel_id=1, source_target_pairs={{0,1},{1,0},{2,3},{3,2},{4,5},{5,4},{6,7},{7,6},{8,9},{9,8},{10,11... | collective-permute-start | bytes 294920 | tf_op jit(solution)/shard_map/ppermute | solution.py:243
